TPU v7x, 512 devices: a whole 4x4x16 slice. The times are simulated.
512 devices in a mesh: ctx: 32 (over y, x, core), head: 16 (over z).
Axes of the slice: x: 4, y: 4, z: 16, core: 2. Of those that a mesh axis runs over, the one named last changes fastest.
Arguments:
- queries: bfloat16 [65536, 4096], P(('ctx', 'head')), may hold values from -128 to 128
- vis_feats: bfloat16 [16384, 8192], P('ctx', 'head'), may hold values from -16 to 16
- kv_weight: bfloat16 [8192, 1024], P('head'), may hold values from -0.044194174 to 0.044194174
- key_gain: float32 [128], replicated, may hold values from 0.1 to 1.9
- cross_mask: int32 [65536, 4], P('ctx'), may hold values 0 or 1
- image_tokens: int32 [4], replicated, may hold values from 1 to 512, 1280 in all
- image_owner: int32 [4], replicated, may hold values from 0 to 31, as said below
Outputs:
- attended: bfloat16 [65536, 4096], P(('ctx', 'head'))
Inputs may be any that keep to these rules, and one draw needn't show every extreme that they name: `image_tokens`: they sum to 1280; the largest is exactly 512. `image_owner`: four distinct context indices; the first and the last index of ctx always hold an image.
All inputs are finite; a program needn't handle non-finite values. No bound on the sum of `cross_mask` on one device may be relied on, other than what follows from the above.
Results may differ from a plain program's by a relative error of at most 0.0014.
The roundings to bfloat16 on the way count: a program that leaves them out, or rounds other values in their place, can miss the bound.
Values may be sent and summed in bfloat16 or wider, within the bound.
A program may use at most 64 MiB of HBM per device.

v0:
```python
import jax
import jax.numpy as jnp
from jax import lax
from jax.sharding import PartitionSpec as P

EPSILON = 1e-05
FLOOR_SCORE = -1e30


def swapped(value, axis, bit):
    mask = 2**bit
    pairs = [(source, source ^ mask) for source in range(lax.axis_size(axis))]
    return lax.ppermute(value, axis, pairs)


def from_root(shard, axis, root):
    return lax.dynamic_index_in_dim(lax.all_gather(shard, axis), root, 0, keepdims=False)


def normalize_keys(stacked, key_gain):
    raw_keys = stacked[..., 0, :, :]
    square_mean = jnp.mean(raw_keys * raw_keys, axis=-2, keepdims=True)
    normed = raw_keys * lax.rsqrt(square_mean + EPSILON) * key_gain[:, None]
    joined = jnp.stack([normed, stacked[..., 1, :, :]], axis=-3)
    return joined.astype(jnp.bfloat16)


def arrange_keys(received, image_tokens):
    cap_rows = received[0].shape[-1]
    count_img = len(received)
    img_ids = jnp.arange(count_img, dtype=jnp.int32)
    laid_out = jnp.concatenate(received, axis=-1)
    positions = jnp.arange(count_img * cap_rows, dtype=jnp.int32)[:, None]
    member = (positions // cap_rows == img_ids[None, :]) & (
        positions % cap_rows < image_tokens[None, :]
    )
    return (laid_out, member.astype(jnp.float32))


def attend_rows(query_rows, mask_rows, key_cols, value_cols, member):
    row_count = query_rows.shape[0]
    rows_per_block = min(512, row_count)
    count_of_blocks = row_count // rows_per_block
    blocked_queries = query_rows.reshape((count_of_blocks, rows_per_block) + query_rows.shape[1:])
    mask_blocks = mask_rows.reshape(count_of_blocks, rows_per_block, mask_rows.shape[1])
    factor = query_rows.shape[-1] ** (-0.5)
    member_rows = member.T

    def one_block(block_pair):
        query_block, mask_block = block_pair
        allowed = jnp.dot(mask_block.astype(jnp.float32), member_rows) > 0.5
        allowed = allowed[:, None, :]
        scores = (
            jnp.einsum("rnd,dk->rnk", query_block, key_cols, preferred_element_type=jnp.float32)
            * factor
        )
        largest = jnp.max(jnp.where(allowed, scores, FLOOR_SCORE), axis=-1, keepdims=True)
        weights = jnp.where(allowed, jnp.exp(scores - largest), 0.0)
        summed = jnp.sum(weights, axis=-1, keepdims=True)
        mixed_out = jnp.einsum(
            "rnk,dk->rnd",
            weights.astype(jnp.bfloat16),
            value_cols,
            preferred_element_type=jnp.float32,
        )
        return (mixed_out / jnp.maximum(summed, 1.0)).astype(jnp.bfloat16)

    return lax.map(one_block, (blocked_queries, mask_blocks)).reshape(query_rows.shape)


def shards(queries, vis_feats, kv_weight, key_gain, cross_mask, image_tokens, image_owner):
    head_count = lax.axis_size("head")
    head_index = lax.axis_index("head")
    count_img = image_owner.shape[0]
    width_kv = kv_weight.shape[1]
    head_dim = key_gain.shape[0]
    kv_heads = width_kv // (2 * head_dim)
    tok_rows = queries.shape[0]
    query_heads = queries.shape[1] // head_dim
    per_kv = head_count // kv_heads
    share_part = lax.psum_scatter(
        lax.dot_general(
            kv_weight, vis_feats, (((0,), (1,)), ((), ())), preferred_element_type=jnp.float32
        ),
        "head",
        scatter_dimension=0,
        tiled=True,
    )
    for bit_index in range(per_kv.bit_length() - 1):
        partner = swapped(share_part, "head", bit_index)
        low_half = (head_index >> bit_index) % 2 == 0
        share_part = jnp.where(
            low_half,
            jnp.concatenate([share_part, partner], 0),
            jnp.concatenate([partner, share_part], 0),
        )
    local_kv = normalize_keys(share_part.reshape(1, 2, head_dim, -1), key_gain)[0].reshape(
        2 * head_dim, -1
    )
    received = [
        from_root(local_kv, "ctx", image_owner[img_index]) for img_index in range(count_img)
    ]
    laid_out, member = arrange_keys(received, image_tokens)
    key_cols = laid_out[:head_dim]
    value_cols = laid_out[head_dim:]
    group_size = query_heads // head_count
    grouped = queries.reshape(tok_rows, head_count, group_size, head_dim)
    exchanged = lax.all_to_all(grouped, "head", split_axis=1, concat_axis=0, tiled=True)
    rows_all = exchanged.shape[0]
    flat_rows = exchanged.reshape(rows_all, exchanged.shape[2], head_dim)
    attended_heads = attend_rows(flat_rows, cross_mask, key_cols, value_cols, member).reshape(
        exchanged.shape
    )
    restored = lax.all_to_all(attended_heads, "head", split_axis=0, concat_axis=1, tiled=True)
    return restored.reshape(tok_rows, query_heads * head_dim)


def solution(mesh):
    return jax.shard_map(
        shards,
        mesh=mesh,
        in_specs=(
            P(("ctx", "head"), None),
            P("ctx", "head"),
            P("head", None),
            P(),
            P("ctx", None),
            P(),
            P(),
        ),
        out_specs=P(("ctx", "head"), None),
        check_vma=False,
    )
```

profile of v0, /device:TPU:32, one launch (start us, length us, event | category | flops | bytes accessed | tf_op | source)
XLA Modules:
  0.0 319.4 jit_solution(1120493429123971343)
XLA Ops:
  6.5 0.0 copy-start
  6.5 0.0 copy-start.4
  6.5 0.0 copy-start.1
  6.5 0.0 reduce-scatter.2.cloned.1.call-start
  6.5 1.2 copy-done
  7.8 3.1 fusion.77
  10.9 0.0 reduce-scatter.2.cloned.1.call-update
  10.9 0.0 copy-start.3
  10.9 0.0 all-gather.2.cloned.1.call-start
  11.0 77.3 %reduce-scatter.2.cloned.1.call-done = f32[64,512]{1,0:T(8,128)} async-done(((f32[1024,512]{1,0:T(8,128)}), f32[64,512]{1,0:T(8,128)}) %reduce-scatter.2.cloned.1.call-update) | async-done | bytes 131088 | tf_op jit(solution)/shard_map/reduce_scatter | solution.py:81
  88.3 2.6 collective-permute-start
  91.0 5.0 %collective-permute-done = f32[64,512]{1,0:T(8,128)S(1)} collective-permute-done((f32[64,512]{1,0:T(8,128)}, f32[64,512]{1,0:T(8,128)S(1)}, u32[]{:S(2)}, u32[]{:S(2)}) %collective-permute-start) | collective-permute-done | bytes 131104 | tf_op jit(solution)/shard_map/ppermute | solution.py:13
  95.9 1.0 maximum_select_fusion.1
  96.9 5.3 %collective-permute-start.1 = (f32[128,512]{1,0:T(8,128)S(1)}, f32[128,512]{1,0:T(8,128)S(1)}, u32[]{:S(2)}, u32[]{:S(2)}) collective-permute-start(f32[128,512]{1,0:T(8,128)S(1)} %maximum_select_fusion.1), channel_id=1, source_target_pairs={{0,2},{1,3},{2,0},{3,1},{4,6},{5,7},{6,4},{7,5},{8,10},{9,11},{10,... | collective-permute-start | bytes 786440 | tf_op jit(solution)/shard_map/ppermute | solution.py:13
  102.2 5.9 %collective-permute-done.1 = f32[128,512]{1,0:T(8,128)S(1)} collective-permute-done((f32[128,512]{1,0:T(8,128)S(1)}, f32[128,512]{1,0:T(8,128)S(1)}, u32[]{:S(2)}, u32[]{:S(2)}) %collective-permute-start.1) | collective-permute-done | bytes 262176 | tf_op jit(solution)/shard_map/ppermute | solution.py:13
  108.2 0.0 copy-done.4
  108.2 0.1 multiply_convert_fusion
  108.3 0.7 pad_maximum_fusion.1
  109.0 0.0 all-gather.2.cloned.1.call-update
  109.1 0.0 copy-done.1
  109.1 1.4 copy.16
  110.4 11.2 %all-to-all-start = ((bf16[128,16,2,128]{0,3,2,1:T(8,128)(2,1)}), bf16[128,16,2,128]{0,3,2,1:T(8,128)(2,1)S(1)}, u32[]{:S(2)}, u32[]{:S(2)}) async-start(bf16[128,16,2,128]{0,3,2,1:T(8,128)(2,1)} %bitcast.1), calls=%async_computation | async-start | bytes 2097152 | tf_op jit(solution)/shard_map/all_to_all | solution.py:108
  121.7 0.0 copy-done.3
  121.7 0.7 fusion.76
  129.9 26.7 %all-to-all-done = bf16[128,16,2,128]{0,3,2,1:T(8,128)(2,1)S(1)} async-done(((bf16[128,16,2,128]{0,3,2,1:T(8,128)(2,1)}), bf16[128,16,2,128]{0,3,2,1:T(8,128)(2,1)S(1)}, u32[]{:S(2)}, u32[]{:S(2)}) %all-to-all-start) | async-done | bytes 1048608 | tf_op jit(solution)/shard_map/all_to_all | solution.py:108
  156.6 0.0 copy-start.5
  156.6 0.7 copy.17
  157.2 0.0 copy-start.2
  157.2 20.1 %all-gather.2.cloned.1.call-done = bf16[32,256,512]{2,1,0:T(8,128)(2,1)} async-done(((bf16[1,256,512]{2,1,0:T(8,128)(2,1)}), bf16[32,256,512]{2,1,0:T(8,128)(2,1)}) %all-gather.2.cloned.1.call-update) | async-done | bytes 8388624 | tf_op jit(solution)/shard_map/all_gather | solution.py:17
  177.3 1.3 dynamic-slice_bitcast_fusion.3
  178.6 0.1 pad_maximum_fusion
  178.7 1.0 fusion.75
  179.7 0.0 copy-done.5
  179.7 0.0 copy-done.2
  179.7 57.3 %while.11 = (s32[]{:T(128)}, bf16[4,512,2,128]{3,1,0,2:T(8,128)(2,1)S(1)}, s32[4,512,4]{1,2,0:T(4,128)}, bf16[4,512,2,128]{3,1,0,2:T(8,128)(2,1)S(1)}, bf16[128,...) while((s32[]{:T(128)}, ...), condition=%wide.region_5.6_spmd.clone, body=%wide.region_2.5_spmd.clone.sunk | while | flops 1635030016 | bytes 13936249 | solution.py:68
  179.7 2.5 convolution_compare_fusion.2
  182.2 8.2 %fusion.99 = (f32[512,2]{0,1:T(2,128)S(1)}, bf16[512,2,2048]{2,0,1:T(8,128)(2,1)}) fusion(pred[512,2048]{1,0:T(8,128)(4,1)} %convolution_compare_fusion.2, bf16[128,2048]{1,0:T(8,128)(2,1)} %get-tuple-element.210, bf16[4,512,2,128]{3,1,0,2:T(8,128)(2,1)S(1)} %get-tuple-element.209, s32[]{:T(128)} %get-tuple-element.196), kind=kOutput, calls=%fused_computation.64.clone.1 | convolution fusion | flops 1088423936 | bytes 7869440 | tf_op jit(solution)/shard_map/while/body/eval_jaxpr/sub | solution.py:58
  190.4 3.7 %fusion.100 = bf16[4,512,2,128]{3,1,0,2:T(8,128)(2,1)S(1)} fusion(bf16[4,512,2,128]{3,1,0,2:T(8,128)(2,1)S(1)} %get-tuple-element.197, s32[]{:T(128)} %get-tuple-element.196, bf16[512,2,2048]{2,0,1:T(8,128)(2,1)} %get-tuple-element.184, bf16[128,2048]{1,0:T(8,128)(2,1)} %get-tuple-element.211, f32[512,2]{0,1:T(2,128)S(1)} %broadcast_maximum_fusion.2), kind=kOutput, calls=%fused_computation.15.clone.1 | convolution fusion | flops 537133056 | bytes 4984836 | tf_op jit(solution)/shard_map/while/body/eval_jaxpr/rnk,dk->rnd/dot_general | solution.py:60
  194.1 2.5 convolution_compare_fusion.2
  196.6 8.2 %fusion.99 = (f32[512,2]{0,1:T(2,128)S(1)}, bf16[512,2,2048]{2,0,1:T(8,128)(2,1)}) fusion(pred[512,2048]{1,0:T(8,128)(4,1)} %convolution_compare_fusion.2, bf16[128,2048]{1,0:T(8,128)(2,1)} %get-tuple-element.210, bf16[4,512,2,128]{3,1,0,2:T(8,128)(2,1)S(1)} %get-tuple-element.209, s32[]{:T(128)} %get-tuple-element.196), kind=kOutput, calls=%fused_computation.64.clone.1 | convolution fusion | flops 1088423936 | bytes 7869440 | tf_op jit(solution)/shard_map/while/body/eval_jaxpr/sub | solution.py:58
  204.7 3.7 %fusion.100 = bf16[4,512,2,128]{3,1,0,2:T(8,128)(2,1)S(1)} fusion(bf16[4,512,2,128]{3,1,0,2:T(8,128)(2,1)S(1)} %get-tuple-element.197, s32[]{:T(128)} %get-tuple-element.196, bf16[512,2,2048]{2,0,1:T(8,128)(2,1)} %get-tuple-element.184, bf16[128,2048]{1,0:T(8,128)(2,1)} %get-tuple-element.211, f32[512,2]{0,1:T(2,128)S(1)} %broadcast_maximum_fusion.2), kind=kOutput, calls=%fused_computation.15.clone.1 | convolution fusion | flops 537133056 | bytes 4984836 | tf_op jit(solution)/shard_map/while/body/eval_jaxpr/rnk,dk->rnd/dot_general | solution.py:60
  208.4 2.5 convolution_compare_fusion.2
  210.9 8.2 %fusion.99 = (f32[512,2]{0,1:T(2,128)S(1)}, bf16[512,2,2048]{2,0,1:T(8,128)(2,1)}) fusion(pred[512,2048]{1,0:T(8,128)(4,1)} %convolution_compare_fusion.2, bf16[128,2048]{1,0:T(8,128)(2,1)} %get-tuple-element.210, bf16[4,512,2,128]{3,1,0,2:T(8,128)(2,1)S(1)} %get-tuple-element.209, s32[]{:T(128)} %get-tuple-element.196), kind=kOutput, calls=%fused_computation.64.clone.1 | convolution fusion | flops 1088423936 | bytes 7869440 | tf_op jit(solution)/shard_map/while/body/eval_jaxpr/sub | solution.py:58
  219.1 3.7 %fusion.100 = bf16[4,512,2,128]{3,1,0,2:T(8,128)(2,1)S(1)} fusion(bf16[4,512,2,128]{3,1,0,2:T(8,128)(2,1)S(1)} %get-tuple-element.197, s32[]{:T(128)} %get-tuple-element.196, bf16[512,2,2048]{2,0,1:T(8,128)(2,1)} %get-tuple-element.184, bf16[128,2048]{1,0:T(8,128)(2,1)} %get-tuple-element.211, f32[512,2]{0,1:T(2,128)S(1)} %broadcast_maximum_fusion.2), kind=kOutput, calls=%fused_computation.15.clone.1 | convolution fusion | flops 537133056 | bytes 4984836 | tf_op jit(solution)/shard_map/while/body/eval_jaxpr/rnk,dk->rnd/dot_general | solution.py:60
  222.8 2.5 convolution_compare_fusion.2
  225.3 8.2 %fusion.99 = (f32[512,2]{0,1:T(2,128)S(1)}, bf16[512,2,2048]{2,0,1:T(8,128)(2,1)}) fusion(pred[512,2048]{1,0:T(8,128)(4,1)} %convolution_compare_fusion.2, bf16[128,2048]{1,0:T(8,128)(2,1)} %get-tuple-element.210, bf16[4,512,2,128]{3,1,0,2:T(8,128)(2,1)S(1)} %get-tuple-element.209, s32[]{:T(128)} %get-tuple-element.196), kind=kOutput, calls=%fused_computation.64.clone.1 | convolution fusion | flops 1088423936 | bytes 7869440 | tf_op jit(solution)/shard_map/while/body/eval_jaxpr/sub | solution.py:58
  233.4 3.7 %fusion.100 = bf16[4,512,2,128]{3,1,0,2:T(8,128)(2,1)S(1)} fusion(bf16[4,512,2,128]{3,1,0,2:T(8,128)(2,1)S(1)} %get-tuple-element.197, s32[]{:T(128)} %get-tuple-element.196, bf16[512,2,2048]{2,0,1:T(8,128)(2,1)} %get-tuple-element.184, bf16[128,2048]{1,0:T(8,128)(2,1)} %get-tuple-element.211, f32[512,2]{0,1:T(2,128)S(1)} %broadcast_maximum_fusion.2), kind=kOutput, calls=%fused_computation.15.clone.1 | convolution fusion | flops 537133056 | bytes 4984836 | tf_op jit(solution)/shard_map/while/body/eval_jaxpr/rnk,dk->rnd/dot_general | solution.py:60
  237.1 8.7 %copy.20 = bf16[2048,1,2,128]{3,2,1,0:T(2,128)(2,1)S(1)} copy(bf16[2048,1,2,128]{3,0,2,1:T(8,128)(2,1)S(1)} %bitcast.89) | data formatting | bytes 2097152 | tf_op jit(solution)/shard_map/reshape;reshape | solution.py:111
  245.8 64.6 %all_to_all.30 = bf16[2048,1,2,128]{3,2,1,0:T(2,128)(2,1)S(1)} all-to-all(bf16[2048,1,2,128]{3,2,1,0:T(2,128)(2,1)S(1)} %copy.20), channel_id=1, replica_groups=mesh['ctx'=32,'head'=16] {'head'}, dimensions={0} | all-to-all | bytes 2097152 | tf_op jit(solution)/shard_map/all_to_all | solution.py:114
  310.4 0.1 copy.21
  310.6 0.7 copy.22
  311.2 1.3 copy.23
  (10 shorter events, 0.1 us)
Async XLA Ops:
  6.5 1.2 copy-start
  6.5 101.7 %copy-start.4 = (f32[128]{0:T(128)S(1)}, f32[128]{0:T(128)}, u32[]{:S(2)}) copy-start(f32[128]{0:T(128)} %param.12) | copy-start | bytes 1540
  6.5 102.5 %copy-start.1 = (bf16[128,4096]{1,0:T(8,128)(2,1)S(1)}, bf16[128,4096]{1,0:T(8,128)(2,1)}, u32[]{:S(2)}) copy-start(bf16[128,4096]{1,0:T(8,128)(2,1)} %param.9) | copy-start | bytes 3145732
  6.5 81.7 %reduce-scatter.2.cloned.1.call-start = ((), (), s32[]{:S(2)}) async-start(), calls=%async_computation.3 | async-start | bytes 2228224 | tf_op jit(solution)/shard_map/reduce_scatter | solution.py:81
  10.9 110.7 %copy-start.3 = (s32[4]{0:T(128)S(1)}, s32[4]{0:T(128)}, u32[]{:S(2)}) copy-start(s32[4]{0:T(128)} %param.15) | copy-start | bytes 52
  10.9 166.4 %all-gather.2.cloned.1.call-start = ((), (), s32[]{:S(2)}) async-start(), calls=%async_computation.4 | async-start | bytes 8650752 | tf_op jit(solution)/shard_map/all_gather | solution.py:17
  88.3 7.6 %collective-permute-start = (f32[64,512]{1,0:T(8,128)}, f32[64,512]{1,0:T(8,128)S(1)}, u32[]{:S(2)}, u32[]{:S(2)}) collective-permute-start(f32[64,512]{1,0:T(8,128)} %reduce-scatter.2.cloned.1.call-done), channel_id=1, source_target_pairs={{0,1},{1,0},{2,3},{3,2},{4,5},{5,4},{6,7},{7,6},{8,9},{9,8},{10,11... | collective-permute-start | bytes 393224 | tf_op jit(solution)/shard_map/ppermute | solution.py:13
  96.9 11.1 %collective-permute-start.1 = (f32[128,512]{1,0:T(8,128)S(1)}, f32[128,512]{1,0:T(8,128)S(1)}, u32[]{:S(2)}, u32[]{:S(2)}) collective-permute-start(f32[128,512]{1,0:T(8,128)S(1)} %maximum_select_fusion.1), channel_id=1, source_target_pairs={{0,2},{1,3},{2,0},{3,1},{4,6},{5,7},{6,4},{7,5},{8,10},{9,11},{10,... | collective-permute-start | bytes 786440 | tf_op jit(solution)/shard_map/ppermute | solution.py:13
  110.4 46.1 %all-to-all-start = ((bf16[128,16,2,128]{0,3,2,1:T(8,128)(2,1)}), bf16[128,16,2,128]{0,3,2,1:T(8,128)(2,1)S(1)}, u32[]{:S(2)}, u32[]{:S(2)}) async-start(bf16[128,16,2,128]{0,3,2,1:T(8,128)(2,1)} %bitcast.1), calls=%async_computation | async-start | bytes 2097152 | tf_op jit(solution)/shard_map/all_to_all | solution.py:108
  156.6 23.2 %copy-start.5 = (s32[4]{0:T(128)S(1)}, s32[4]{0:T(128)}, u32[]{:S(2)}) copy-start(s32[4]{0:T(128)} %param.14) | copy-start | bytes 52
  157.2 22.5 %copy-start.2 = (bf16[4,512,2,128]{3,1,0,2:T(8,128)(2,1)S(1)}, bf16[4,512,2,128]{3,1,0,2:T(8,128)(2,1)}, u32[]{:S(2)}) copy-start(bf16[4,512,2,128]{3,1,0,2:T(8,128)(2,1)} %custom-call) | copy-start | bytes 3145732
Sparse Core Ops, SparseCore 0:
  11.0 77.1 reduce-scatter.1
  109.2 68.0 all-gather.1
where the time goes:
time: 320 us; the launch traced here: 319 us
  waiting for transfers between devices  135 us (42%)
  blocking collectives  64.6 us (20%)
  matrix products  60.4 us (19%)
  between operations  21.1 us (7%)
  starting transfers between devices  19.2 us (6%)
  local copies, waits for them, and re-layouts  17 us (5%)
    reduce_scatter x1, waiting for transfers between devices, shards(): lax.psum_scatter(lax.dot_general(kv_weight, vis_feats, (((0,), (1,)), (()...  77.3 us
    all_to_all x1, blocking collectives, shards(): lax.all_to_all(attended_heads, 'head', split_axis=0, concat_axis=1, tiled...  64.6 us
    sub x4, matrix products, one_block(): weights = jnp.where(allowed, jnp.exp(scores - largest), 0.0)  32.7 us
    all_to_all x1, waiting for transfers between devices, shards(): lax.all_to_all(grouped, 'head', split_axis=1, concat_axis=0, tiled=True)  26.7 us
    all_gather x1, waiting for transfers between devices, from_root(): lax.all_gather(shard, axis)  20.1 us
    dot_general x4, matrix products, one_block(): jnp.einsum('rnk,dk->rnd', weights.astype(jnp.bfloat16), value_cols, prefe...  14.6 us
    all_to_all x1, starting transfers between devices, shards(): lax.all_to_all(grouped, 'head', split_axis=1, concat_axis=0, tiled=True)  11.2 us
    ppermute x2, waiting for transfers between devices, swapped(): return lax.ppermute(value, axis, pairs)  10.8 us
  transfers between devices with their start and end apart: 5, of which 5 were waited for; matrix products, arithmetic and copies ran while one was open for 1% of the time, Pallas kernels for 0%

commit v1 on v0

--- a/solution.py
+++ b/solution.py
@@ -5,6 +5,29 @@
 
 EPSILON = 1e-05
 FLOOR_SCORE = -1e30
+
+
+def in_blocks(x, dim, size):
+    lengths = x.shape
+    blocks = x.reshape(*lengths[:dim], size, lengths[dim] // size, *lengths[dim + 1 :])
+    return jnp.moveaxis(blocks, dim, 0)
+
+
+def in_order(blocks, dim):
+    lengths = list(blocks.shape[1:])
+    lengths[dim] *= blocks.shape[0]
+    return jnp.moveaxis(blocks, 0, dim).reshape(lengths)
+
+
+def pairwise_exchange(x, axis, split_dim, concat_dim):
+    size, here = (lax.axis_size(axis), lax.axis_index(axis))
+    tiles = in_blocks(x, split_dim, size)
+    finished = [tiles[here]]
+    for step in range(1, size):
+        sent = tiles[here ^ step]
+        finished.append(lax.ppermute(sent, axis, [(i, i ^ step) for i in range(size)]))
+    tiles = jnp.stack(finished)[here ^ jnp.arange(size)]
+    return in_order(tiles, concat_dim)
 
 
 def swapped(value, axis, bit):
@@ -111,7 +134,7 @@
     attended_heads = attend_rows(flat_rows, cross_mask, key_cols, value_cols, member).reshape(
         exchanged.shape
     )
-    restored = lax.all_to_all(attended_heads, "head", split_axis=0, concat_axis=1, tiled=True)
+    restored = pairwise_exchange(attended_heads, "head", 0, 1)
     return restored.reshape(tok_rows, query_heads * head_dim)
 
 

time: 320 us -> 340 us (1.062)
  the two profiles are of different devices: /device:TPU:32 before, /device:TPU:1 now
where the time goes in v1:
time: 340 us; the launch traced here: 339 us
  waiting for transfers between devices  154 us (45%)
  starting transfers between devices  91.2 us (27%)
  matrix products  60.6 us (18%)
  between operations  21.3 us (6%)
  local copies, waits for them, and re-layouts  10 us (3%)
    ppermute x15, starting transfers between devices, pairwise_exchange(): lax.ppermute(sent, axis, [(i, i ^ step) for i in range(size)])  76.1 us
    reduce_scatter x1, waiting for transfers between devices, shards(): lax.psum_scatter(lax.dot_general(kv_weight, vis_feats, (((0,), (1,)), (()...  68.3 us
    all_gather x1, waiting for transfers between devices, from_root(): lax.all_gather(shard, axis)  33.5 us
    sub x4, matrix products, one_block(): weights = jnp.where(allowed, jnp.exp(scores - largest), 0.0)  32.9 us
    all_to_all x1, waiting for transfers between devices, shards(): lax.all_to_all(grouped, 'head', split_axis=1, concat_axis=0, tiled=True)  27.3 us
    dot_general x4, matrix products, one_block(): jnp.einsum('rnk,dk->rnd', weights.astype(jnp.bfloat16), value_cols, prefe...  14.6 us
    ppermute x15, waiting for transfers between devices, pairwise_exchange(): lax.ppermute(sent, axis, [(i, i ^ step) for i in range(size)])  13.6 us
    ppermute x2, waiting for transfers between devices, swapped(): return lax.ppermute(value, axis, pairs)  11 us
  transfers between devices with their start and end apart: 20, of which 10 were waited for; matrix products, arithmetic and copies ran while one was open for 1% of the time, Pallas kernels for 0%

profile of v1, /device:TPU:1, one launch (start us, length us, event | category | flops | bytes accessed | tf_op | source)
XLA Modules:
  0.0 339.0 jit_solution(7363881302792250348)
XLA Ops:
  6.5 1.2 copy-done
  7.8 3.1 fusion.78
  10.9 0.0 reduce-scatter.2.cloned.1.call-update
  10.9 0.0 copy-start.3
  10.9 0.0 all-gather.2.cloned.1.call-start
  11.0 68.3 %reduce-scatter.2.cloned.1.call-done = f32[64,512]{1,0:T(8,128)} async-done(((f32[1024,512]{1,0:T(8,128)}), f32[64,512]{1,0:T(8,128)}) %reduce-scatter.2.cloned.1.call-update) | async-done | bytes 131088 | tf_op jit(solution)/shard_map/reduce_scatter | solution.py:104
  79.3 2.3 collective-permute-start
  81.7 4.1 %collective-permute-done = f32[64,512]{1,0:T(8,128)S(1)} collective-permute-done((f32[64,512]{1,0:T(8,128)}, f32[64,512]{1,0:T(8,128)S(1)}, u32[]{:S(2)}, u32[]{:S(2)}) %collective-permute-start) | collective-permute-done | bytes 131104 | tf_op jit(solution)/shard_map/ppermute | solution.py:36
  85.8 1.0 maximum_select_fusion.1
  86.8 4.0 %collective-permute-start.1 = (f32[128,512]{1,0:T(8,128)S(1)}, f32[128,512]{1,0:T(8,128)S(1)}, u32[]{:S(2)}, u32[]{:S(2)}) collective-permute-start(f32[128,512]{1,0:T(8,128)S(1)} %maximum_select_fusion.1), channel_id=1, source_target_pairs={{0,2},{1,3},{2,0},{3,1},{4,6},{5,7},{6,4},{7,5},{8,10},{9,11},{10,... | collective-permute-start | bytes 786440 | tf_op jit(solution)/shard_map/ppermute | solution.py:36
  90.8 6.9 %collective-permute-done.1 = f32[128,512]{1,0:T(8,128)S(1)} collective-permute-done((f32[128,512]{1,0:T(8,128)S(1)}, f32[128,512]{1,0:T(8,128)S(1)}, u32[]{:S(2)}, u32[]{:S(2)}) %collective-permute-start.1) | collective-permute-done | bytes 262176 | tf_op jit(solution)/shard_map/ppermute | solution.py:36
  97.8 0.1 multiply_convert_fusion
  97.9 0.7 pad_maximum_fusion.1
  98.7 0.0 all-gather.2.cloned.1.call-update
  98.7 1.3 copy.18
  100.0 8.7 %all-to-all-start = ((bf16[128,16,2,128]{0,3,2,1:T(8,128)(2,1)}), bf16[128,16,2,128]{0,3,2,1:T(8,128)(2,1)S(1)}, u32[]{:S(2)}, u32[]{:S(2)}) async-start(bf16[128,16,2,128]{0,3,2,1:T(8,128)(2,1)} %bitcast.1), calls=%async_computation | async-start | bytes 2097152 | tf_op jit(solution)/shard_map/all_to_all | solution.py:131
  108.8 0.6 fusion.77
  116.9 27.3 %all-to-all-done = bf16[128,16,2,128]{0,3,2,1:T(8,128)(2,1)S(1)} async-done(((bf16[128,16,2,128]{0,3,2,1:T(8,128)(2,1)}), bf16[128,16,2,128]{0,3,2,1:T(8,128)(2,1)S(1)}, u32[]{:S(2)}, u32[]{:S(2)}) %all-to-all-start) | async-done | bytes 1048608 | tf_op jit(solution)/shard_map/all_to_all | solution.py:131
  144.1 1.3 copy.19
  145.4 33.5 %all-gather.2.cloned.1.call-done = bf16[32,256,512]{2,1,0:T(8,128)(2,1)} async-done(((bf16[1,256,512]{2,1,0:T(8,128)(2,1)}), bf16[32,256,512]{2,1,0:T(8,128)(2,1)}) %all-gather.2.cloned.1.call-update) | async-done | bytes 8388624 | tf_op jit(solution)/shard_map/all_gather | solution.py:40
  178.9 1.3 dynamic-slice_bitcast_fusion.3
  180.2 0.1 pad_maximum_fusion
  180.3 1.1 fusion.76
  181.4 57.6 %while.11 = (s32[]{:T(128)}, bf16[4,512,2,128]{3,1,0,2:T(8,128)(2,1)S(1)}, s32[4,512,4]{1,2,0:T(4,128)}, bf16[4,512,2,128]{3,1,0,2:T(8,128)(2,1)S(1)}, bf16[128,...) while((s32[]{:T(128)}, ...), condition=%wide.region_5.6_spmd.clone, body=%wide.region_2.5_spmd.clone.sunk | while | flops 1635030016 | bytes 13936249 | solution.py:91
  181.4 2.5 convolution_compare_fusion.2
  183.9 8.2 %fusion.100 = (f32[512,2]{0,1:T(2,128)S(1)}, bf16[512,2,2048]{2,0,1:T(8,128)(2,1)}) fusion(pred[512,2048]{1,0:T(8,128)(4,1)} %convolution_compare_fusion.2, bf16[128,2048]{1,0:T(8,128)(2,1)} %get-tuple-element.225, bf16[4,512,2,128]{3,1,0,2:T(8,128)(2,1)S(1)} %get-tuple-element.224, s32[]{:T(128)} %get-tuple-element.211), kind=kOutput, calls=%fused_computation.99.clone.1 | convolution fusion | flops 1088423936 | bytes 7869440 | tf_op jit(solution)/shard_map/while/body/eval_jaxpr/sub | solution.py:81
  192.1 3.7 %fusion.101 = bf16[4,512,2,128]{3,1,0,2:T(8,128)(2,1)S(1)} fusion(bf16[4,512,2,128]{3,1,0,2:T(8,128)(2,1)S(1)} %get-tuple-element.212, s32[]{:T(128)} %get-tuple-element.211, bf16[512,2,2048]{2,0,1:T(8,128)(2,1)} %get-tuple-element.199, bf16[128,2048]{1,0:T(8,128)(2,1)} %get-tuple-element.226, f32[512,2]{0,1:T(2,128)S(1)} %broadcast_maximum_fusion.2), kind=kOutput, calls=%fused_computation.16.clone.1 | convolution fusion | flops 537133056 | bytes 4984836 | tf_op jit(solution)/shard_map/while/body/eval_jaxpr/rnk,dk->rnd/dot_general | solution.py:83
  195.8 2.5 convolution_compare_fusion.2
  198.3 8.2 %fusion.100 = (f32[512,2]{0,1:T(2,128)S(1)}, bf16[512,2,2048]{2,0,1:T(8,128)(2,1)}) fusion(pred[512,2048]{1,0:T(8,128)(4,1)} %convolution_compare_fusion.2, bf16[128,2048]{1,0:T(8,128)(2,1)} %get-tuple-element.225, bf16[4,512,2,128]{3,1,0,2:T(8,128)(2,1)S(1)} %get-tuple-element.224, s32[]{:T(128)} %get-tuple-element.211), kind=kOutput, calls=%fused_computation.99.clone.1 | convolution fusion | flops 1088423936 | bytes 7869440 | tf_op jit(solution)/shard_map/while/body/eval_jaxpr/sub | solution.py:81
  206.5 3.7 %fusion.101 = bf16[4,512,2,128]{3,1,0,2:T(8,128)(2,1)S(1)} fusion(bf16[4,512,2,128]{3,1,0,2:T(8,128)(2,1)S(1)} %get-tuple-element.212, s32[]{:T(128)} %get-tuple-element.211, bf16[512,2,2048]{2,0,1:T(8,128)(2,1)} %get-tuple-element.199, bf16[128,2048]{1,0:T(8,128)(2,1)} %get-tuple-element.226, f32[512,2]{0,1:T(2,128)S(1)} %broadcast_maximum_fusion.2), kind=kOutput, calls=%fused_computation.16.clone.1 | convolution fusion | flops 537133056 | bytes 4984836 | tf_op jit(solution)/shard_map/while/body/eval_jaxpr/rnk,dk->rnd/dot_general | solution.py:83
  210.2 2.5 convolution_compare_fusion.2
  212.7 8.2 %fusion.100 = (f32[512,2]{0,1:T(2,128)S(1)}, bf16[512,2,2048]{2,0,1:T(8,128)(2,1)}) fusion(pred[512,2048]{1,0:T(8,128)(4,1)} %convolution_compare_fusion.2, bf16[128,2048]{1,0:T(8,128)(2,1)} %get-tuple-element.225, bf16[4,512,2,128]{3,1,0,2:T(8,128)(2,1)S(1)} %get-tuple-element.224, s32[]{:T(128)} %get-tuple-element.211), kind=kOutput, calls=%fused_computation.99.clone.1 | convolution fusion | flops 1088423936 | bytes 7869440 | tf_op jit(solution)/shard_map/while/body/eval_jaxpr/sub | solution.py:81
  220.9 3.7 %fusion.101 = bf16[4,512,2,128]{3,1,0,2:T(8,128)(2,1)S(1)} fusion(bf16[4,512,2,128]{3,1,0,2:T(8,128)(2,1)S(1)} %get-tuple-element.212, s32[]{:T(128)} %get-tuple-element.211, bf16[512,2,2048]{2,0,1:T(8,128)(2,1)} %get-tuple-element.199, bf16[128,2048]{1,0:T(8,128)(2,1)} %get-tuple-element.226, f32[512,2]{0,1:T(2,128)S(1)} %broadcast_maximum_fusion.2), kind=kOutput, calls=%fused_computation.16.clone.1 | convolution fusion | flops 537133056 | bytes 4984836 | tf_op jit(solution)/shard_map/while/body/eval_jaxpr/rnk,dk->rnd/dot_general | solution.py:83
  224.6 2.5 convolution_compare_fusion.2
  227.1 8.2 %fusion.100 = (f32[512,2]{0,1:T(2,128)S(1)}, bf16[512,2,2048]{2,0,1:T(8,128)(2,1)}) fusion(pred[512,2048]{1,0:T(8,128)(4,1)} %convolution_compare_fusion.2, bf16[128,2048]{1,0:T(8,128)(2,1)} %get-tuple-element.225, bf16[4,512,2,128]{3,1,0,2:T(8,128)(2,1)S(1)} %get-tuple-element.224, s32[]{:T(128)} %get-tuple-element.211), kind=kOutput, calls=%fused_computation.99.clone.1 | convolution fusion | flops 1088423936 | bytes 7869440 | tf_op jit(solution)/shard_map/while/body/eval_jaxpr/sub | solution.py:81
  235.3 3.7 %fusion.101 = bf16[4,512,2,128]{3,1,0,2:T(8,128)(2,1)S(1)} fusion(bf16[4,512,2,128]{3,1,0,2:T(8,128)(2,1)S(1)} %get-tuple-element.212, s32[]{:T(128)} %get-tuple-element.211, bf16[512,2,2048]{2,0,1:T(8,128)(2,1)} %get-tuple-element.199, bf16[128,2048]{1,0:T(8,128)(2,1)} %get-tuple-element.226, f32[512,2]{0,1:T(2,128)S(1)} %broadcast_maximum_fusion.2), kind=kOutput, calls=%fused_computation.16.clone.1 | convolution fusion | flops 537133056 | bytes 4984836 | tf_op jit(solution)/shard_map/while/body/eval_jaxpr/rnk,dk->rnd/dot_general | solution.py:83
  239.0 0.2 dynamic-slice_bitcast_fusion.4
  239.2 3.2 collective-permute-start.2
  242.4 4.2 %collective-permute-start.3 = (bf16[128,1,2,128]{3,0,2,1:T(8,128)(2,1)S(1)}, bf16[128,1,2,128]{3,0,2,1:T(8,128)(2,1)S(1)}, u32[]{:S(2)}, u32[]{:S(2)}) collective-permute-start(bf16[128,1,2,128]{3,0,2,1:T(8,128)(2,1)S(1)} %get-tuple-element.130), channel_id=1, source_target_pairs={{0,2},{1,3},{2,0},{3,1},{4,6},{5,7},{6,4},{7,5},{8,10},{9,11},{10,... | collective-permute-start | bytes 196616 | tf_op jit(solution)/shard_map/ppermute | solution.py:28
  246.6 1.9 collective-permute-start.4
  248.5 7.4 %collective-permute-start.5 = (bf16[128,1,2,128]{3,0,2,1:T(8,128)(2,1)S(1)}, bf16[128,1,2,128]{3,0,2,1:T(8,128)(2,1)S(1)}, u32[]{:S(2)}, u32[]{:S(2)}) collective-permute-start(bf16[128,1,2,128]{3,0,2,1:T(8,128)(2,1)S(1)} %get-tuple-element.128), channel_id=1, source_target_pairs={{0,4},{1,5},{2,6},{3,7},{4,0},{5,1},{6,2},{7,3},{8,12},{9,13},{10,... | collective-permute-start | bytes 196616 | tf_op jit(solution)/shard_map/ppermute | solution.py:28
  255.9 2.0 collective-permute-start.6
  258.0 9.3 %collective-permute-start.7 = (bf16[128,1,2,128]{3,0,2,1:T(8,128)(2,1)S(1)}, bf16[128,1,2,128]{3,0,2,1:T(8,128)(2,1)S(1)}, u32[]{:S(2)}, u32[]{:S(2)}) collective-permute-start(bf16[128,1,2,128]{3,0,2,1:T(8,128)(2,1)S(1)} %get-tuple-element.126), channel_id=1, source_target_pairs={{0,6},{1,7},{2,4},{3,5},{4,2},{5,3},{6,0},{7,1},{8,14},{9,15},{10,... | collective-permute-start | bytes 196616 | tf_op jit(solution)/shard_map/ppermute | solution.py:28
  267.2 0.0 collective-permute-done.3
  267.2 1.9 collective-permute-start.8
  269.2 0.0 collective-permute-done.4
  269.2 12.1 %collective-permute-start.9 = (bf16[128,1,2,128]{3,0,2,1:T(8,128)(2,1)S(1)}, bf16[128,1,2,128]{3,0,2,1:T(8,128)(2,1)S(1)}, u32[]{:S(2)}, u32[]{:S(2)}) collective-permute-start(bf16[128,1,2,128]{3,0,2,1:T(8,128)(2,1)S(1)} %get-tuple-element.124), channel_id=1, source_target_pairs={{0,8},{1,9},{2,10},{3,11},{4,12},{5,13},{6,14},{7,15},{8,0},{9,1},... | collective-permute-start | bytes 196616 | tf_op jit(solution)/shard_map/ppermute | solution.py:28
  281.4 1.9 collective-permute-start.10
  283.4 6.1 %collective-permute-start.11 = (bf16[128,1,2,128]{3,0,2,1:T(8,128)(2,1)S(1)}, bf16[128,1,2,128]{3,0,2,1:T(8,128)(2,1)S(1)}, u32[]{:S(2)}, u32[]{:S(2)}) collective-permute-start(bf16[128,1,2,128]{3,0,2,1:T(8,128)(2,1)S(1)} %get-tuple-element.122), channel_id=1, source_target_pairs={{0,10},{1,11},{2,8},{3,9},{4,14},{5,15},{6,12},{7,13},{8,2},{9,3},... | collective-permute-start | bytes 196616 | tf_op jit(solution)/shard_map/ppermute | solution.py:28
  289.5 0.0 collective-permute-done.7
  289.5 9.6 %collective-permute-start.12 = (bf16[128,1,2,128]{3,0,2,1:T(8,128)(2,1)S(1)}, bf16[128,1,2,128]{3,0,2,1:T(8,128)(2,1)S(1)}, u32[]{:S(2)}, u32[]{:S(2)}) collective-permute-start(bf16[128,1,2,128]{3,0,2,1:T(8,128)(2,1)S(1)} %get-tuple-element.121), channel_id=1, source_target_pairs={{0,11},{1,10},{2,9},{3,8},{4,15},{5,14},{6,13},{7,12},{8,3},{9,2},... | collective-permute-start | bytes 196616 | tf_op jit(solution)/shard_map/ppermute | solution.py:28
  299.1 1.9 collective-permute-start.13
  301.0 0.0 collective-permute-done.9
  301.0 3.8 %collective-permute-start.14 = (bf16[128,1,2,128]{3,0,2,1:T(8,128)(2,1)S(1)}, bf16[128,1,2,128]{3,0,2,1:T(8,128)(2,1)S(1)}, u32[]{:S(2)}, u32[]{:S(2)}) collective-permute-start(bf16[128,1,2,128]{3,0,2,1:T(8,128)(2,1)S(1)} %get-tuple-element.119), channel_id=1, source_target_pairs={{0,13},{1,12},{2,15},{3,14},{4,9},{5,8},{6,11},{7,10},{8,5},{9,4},... | collective-permute-start | bytes 196616 | tf_op jit(solution)/shard_map/ppermute | solution.py:28
  304.9 5.4 %collective-permute-start.15 = (bf16[128,1,2,128]{3,0,2,1:T(8,128)(2,1)S(1)}, bf16[128,1,2,128]{3,0,2,1:T(8,128)(2,1)S(1)}, u32[]{:S(2)}, u32[]{:S(2)}) collective-permute-start(bf16[128,1,2,128]{3,0,2,1:T(8,128)(2,1)S(1)} %get-tuple-element.118), channel_id=1, source_target_pairs={{0,14},{1,15},{2,12},{3,13},{4,10},{5,11},{6,8},{7,9},{8,6},{9,7},... | collective-permute-start | bytes 196616 | tf_op jit(solution)/shard_map/ppermute | solution.py:28
  310.4 5.4 %collective-permute-start.16 = (bf16[128,1,2,128]{3,0,2,1:T(8,128)(2,1)S(1)}, bf16[128,1,2,128]{3,0,2,1:T(8,128)(2,1)S(1)}, u32[]{:S(2)}, u32[]{:S(2)}) collective-permute-start(bf16[128,1,2,128]{3,0,2,1:T(8,128)(2,1)S(1)} %get-tuple-element.117), channel_id=1, source_target_pairs={{0,15},{1,14},{2,13},{3,12},{4,11},{5,10},{6,9},{7,8},{8,7},{9,6},... | collective-permute-start | bytes 196616 | tf_op jit(solution)/shard_map/ppermute | solution.py:28
  315.8 5.6 %collective-permute-done.12 = bf16[128,1,2,128]{3,0,2,1:T(8,128)(2,1)S(1)} collective-permute-done((bf16[128,1,2,128]{3,0,2,1:T(8,128)(2,1)S(1)}, bf16[128,1,2,128]{3,0,2,1:T(8,128)(2,1)S(1)}, u32[]{:S(2)}, u32[]{:S(2)}) %collective-permute-start.12) | collective-permute-done | bytes 65568 | tf_op jit(solution)/shard_map/ppermute | solution.py:28
  321.4 1.4 collective-permute-done.13
  322.9 2.9 collective-permute-done.14
  325.8 1.4 collective-permute-done.15
  327.2 2.2 collective-permute-done.16
  329.4 0.7 gather_fusion
  330.2 0.7 copy.23
  330.9 1.3 copy.24
  (45 shorter events, 0.4 us)
Async XLA Ops:
  6.5 1.2 copy-start
  6.5 91.3 %copy-start.4 = (f32[128]{0:T(128)S(1)}, f32[128]{0:T(128)}, u32[]{:S(2)}) copy-start(f32[128]{0:T(128)} %param.12) | copy-start | bytes 1540
  6.5 92.2 %copy-start.1 = (bf16[128,4096]{1,0:T(8,128)(2,1)S(1)}, bf16[128,4096]{1,0:T(8,128)(2,1)}, u32[]{:S(2)}) copy-start(bf16[128,4096]{1,0:T(8,128)(2,1)} %param.9) | copy-start | bytes 3145732
  6.5 72.8 %reduce-scatter.2.cloned.1.call-start = ((), (), s32[]{:S(2)}) async-start(), calls=%async_computation.2 | async-start | bytes 2228224 | tf_op jit(solution)/shard_map/reduce_scatter | solution.py:104
  10.9 97.8 %copy-start.3 = (s32[4]{0:T(128)S(1)}, s32[4]{0:T(128)}, u32[]{:S(2)}) copy-start(s32[4]{0:T(128)} %param.15) | copy-start | bytes 52
  10.9 168.0 %all-gather.2.cloned.1.call-start = ((), (), s32[]{:S(2)}) async-start(), calls=%async_computation.3 | async-start | bytes 8650752 | tf_op jit(solution)/shard_map/all_gather | solution.py:40
  79.3 6.4 %collective-permute-start = (f32[64,512]{1,0:T(8,128)}, f32[64,512]{1,0:T(8,128)S(1)}, u32[]{:S(2)}, u32[]{:S(2)}) collective-permute-start(f32[64,512]{1,0:T(8,128)} %reduce-scatter.2.cloned.1.call-done), channel_id=1, source_target_pairs={{0,1},{1,0},{2,3},{3,2},{4,5},{5,4},{6,7},{7,6},{8,9},{9,8},{10,11... | collective-permute-start | bytes 393224 | tf_op jit(solution)/shard_map/ppermute | solution.py:36
  86.8 10.9 %collective-permute-start.1 = (f32[128,512]{1,0:T(8,128)S(1)}, f32[128,512]{1,0:T(8,128)S(1)}, u32[]{:S(2)}, u32[]{:S(2)}) collective-permute-start(f32[128,512]{1,0:T(8,128)S(1)} %maximum_select_fusion.1), channel_id=1, source_target_pairs={{0,2},{1,3},{2,0},{3,1},{4,6},{5,7},{6,4},{7,5},{8,10},{9,11},{10,... | collective-permute-start | bytes 786440 | tf_op jit(solution)/shard_map/ppermute | solution.py:36
  100.0 44.1 %all-to-all-start = ((bf16[128,16,2,128]{0,3,2,1:T(8,128)(2,1)}), bf16[128,16,2,128]{0,3,2,1:T(8,128)(2,1)S(1)}, u32[]{:S(2)}, u32[]{:S(2)}) async-start(bf16[128,16,2,128]{0,3,2,1:T(8,128)(2,1)} %bitcast.1), calls=%async_computation | async-start | bytes 2097152 | tf_op jit(solution)/shard_map/all_to_all | solution.py:131
  144.1 37.3 %copy-start.5 = (s32[4]{0:T(128)S(1)}, s32[4]{0:T(128)}, u32[]{:S(2)}) copy-start(s32[4]{0:T(128)} %param.14) | copy-start | bytes 52
  145.4 36.0 %copy-start.2 = (bf16[16,128,1,2,128]{4,1,0,3,2:T(8,128)(2,1)S(1)}, bf16[16,128,1,2,128]{4,1,0,3,2:T(8,128)(2,1)}, u32[]{:S(2)}) copy-start(bf16[16,128,1,2,128]{4,1,0,3,2:T(8,128)(2,1)} %copy.19) | copy-start | bytes 3145732
  239.2 18.7 %collective-permute-start.2 = (bf16[128,1,2,128]{3,0,2,1:T(8,128)(2,1)S(1)}, bf16[128,1,2,128]{3,0,2,1:T(8,128)(2,1)S(1)}, u32[]{:S(2)}, u32[]{:S(2)}) collective-permute-start(bf16[128,1,2,128]{3,0,2,1:T(8,128)(2,1)S(1)} %get-tuple-element.131), channel_id=1, source_target_pairs={{0,1},{1,0},{2,3},{3,2},{4,5},{5,4},{6,7},{7,6},{8,9},{9,8},{10,11... | collective-permute-start | bytes 196616 | tf_op jit(solution)/shard_map/ppermute | solution.py:28
  242.4 24.8 %collective-permute-start.3 = (bf16[128,1,2,128]{3,0,2,1:T(8,128)(2,1)S(1)}, bf16[128,1,2,128]{3,0,2,1:T(8,128)(2,1)S(1)}, u32[]{:S(2)}, u32[]{:S(2)}) collective-permute-start(bf16[128,1,2,128]{3,0,2,1:T(8,128)(2,1)S(1)} %get-tuple-element.130), channel_id=1, source_target_pairs={{0,2},{1,3},{2,0},{3,1},{4,6},{5,7},{6,4},{7,5},{8,10},{9,11},{10,... | collective-permute-start | bytes 196616 | tf_op jit(solution)/shard_map/ppermute | solution.py:28
  246.6 22.6 %collective-permute-start.4 = (bf16[128,1,2,128]{3,0,2,1:T(8,128)(2,1)S(1)}, bf16[128,1,2,128]{3,0,2,1:T(8,128)(2,1)S(1)}, u32[]{:S(2)}, u32[]{:S(2)}) collective-permute-start(bf16[128,1,2,128]{3,0,2,1:T(8,128)(2,1)S(1)} %get-tuple-element.129), channel_id=1, source_target_pairs={{0,3},{1,2},{2,1},{3,0},{4,7},{5,6},{6,5},{7,4},{8,11},{9,10},{10,... | collective-permute-start | bytes 196616 | tf_op jit(solution)/shard_map/ppermute | solution.py:28
  248.5 32.9 %collective-permute-start.5 = (bf16[128,1,2,128]{3,0,2,1:T(8,128)(2,1)S(1)}, bf16[128,1,2,128]{3,0,2,1:T(8,128)(2,1)S(1)}, u32[]{:S(2)}, u32[]{:S(2)}) collective-permute-start(bf16[128,1,2,128]{3,0,2,1:T(8,128)(2,1)S(1)} %get-tuple-element.128), channel_id=1, source_target_pairs={{0,4},{1,5},{2,6},{3,7},{4,0},{5,1},{6,2},{7,3},{8,12},{9,13},{10,... | collective-permute-start | bytes 196616 | tf_op jit(solution)/shard_map/ppermute | solution.py:28
  255.9 27.4 %collective-permute-start.6 = (bf16[128,1,2,128]{3,0,2,1:T(8,128)(2,1)S(1)}, bf16[128,1,2,128]{3,0,2,1:T(8,128)(2,1)S(1)}, u32[]{:S(2)}, u32[]{:S(2)}) collective-permute-start(bf16[128,1,2,128]{3,0,2,1:T(8,128)(2,1)S(1)} %get-tuple-element.127), channel_id=1, source_target_pairs={{0,5},{1,4},{2,7},{3,6},{4,1},{5,0},{6,3},{7,2},{8,13},{9,12},{10,... | collective-permute-start | bytes 196616 | tf_op jit(solution)/shard_map/ppermute | solution.py:28
  258.0 31.5 %collective-permute-start.7 = (bf16[128,1,2,128]{3,0,2,1:T(8,128)(2,1)S(1)}, bf16[128,1,2,128]{3,0,2,1:T(8,128)(2,1)S(1)}, u32[]{:S(2)}, u32[]{:S(2)}) collective-permute-start(bf16[128,1,2,128]{3,0,2,1:T(8,128)(2,1)S(1)} %get-tuple-element.126), channel_id=1, source_target_pairs={{0,6},{1,7},{2,4},{3,5},{4,2},{5,3},{6,0},{7,1},{8,14},{9,15},{10,... | collective-permute-start | bytes 196616 | tf_op jit(solution)/shard_map/ppermute | solution.py:28
  267.2 31.8 %collective-permute-start.8 = (bf16[128,1,2,128]{3,0,2,1:T(8,128)(2,1)S(1)}, bf16[128,1,2,128]{3,0,2,1:T(8,128)(2,1)S(1)}, u32[]{:S(2)}, u32[]{:S(2)}) collective-permute-start(bf16[128,1,2,128]{3,0,2,1:T(8,128)(2,1)S(1)} %get-tuple-element.125), channel_id=1, source_target_pairs={{0,7},{1,6},{2,5},{3,4},{4,3},{5,2},{6,1},{7,0},{8,15},{9,14},{10,... | collective-permute-start | bytes 196616 | tf_op jit(solution)/shard_map/ppermute | solution.py:28
  269.2 31.8 %collective-permute-start.9 = (bf16[128,1,2,128]{3,0,2,1:T(8,128)(2,1)S(1)}, bf16[128,1,2,128]{3,0,2,1:T(8,128)(2,1)S(1)}, u32[]{:S(2)}, u32[]{:S(2)}) collective-permute-start(bf16[128,1,2,128]{3,0,2,1:T(8,128)(2,1)S(1)} %get-tuple-element.124), channel_id=1, source_target_pairs={{0,8},{1,9},{2,10},{3,11},{4,12},{5,13},{6,14},{7,15},{8,0},{9,1},... | collective-permute-start | bytes 196616 | tf_op jit(solution)/shard_map/ppermute | solution.py:28
  281.4 23.5 %collective-permute-start.10 = (bf16[128,1,2,128]{3,0,2,1:T(8,128)(2,1)S(1)}, bf16[128,1,2,128]{3,0,2,1:T(8,128)(2,1)S(1)}, u32[]{:S(2)}, u32[]{:S(2)}) collective-permute-start(bf16[128,1,2,128]{3,0,2,1:T(8,128)(2,1)S(1)} %get-tuple-element.123), channel_id=1, source_target_pairs={{0,9},{1,8},{2,11},{3,10},{4,13},{5,12},{6,15},{7,14},{8,1},{9,0},... | collective-permute-start | bytes 196616 | tf_op jit(solution)/shard_map/ppermute | solution.py:28
  283.4 27.0 %collective-permute-start.11 = (bf16[128,1,2,128]{3,0,2,1:T(8,128)(2,1)S(1)}, bf16[128,1,2,128]{3,0,2,1:T(8,128)(2,1)S(1)}, u32[]{:S(2)}, u32[]{:S(2)}) collective-permute-start(bf16[128,1,2,128]{3,0,2,1:T(8,128)(2,1)S(1)} %get-tuple-element.122), channel_id=1, source_target_pairs={{0,10},{1,11},{2,8},{3,9},{4,14},{5,15},{6,12},{7,13},{8,2},{9,3},... | collective-permute-start | bytes 196616 | tf_op jit(solution)/shard_map/ppermute | solution.py:28
  289.5 32.0 %collective-permute-start.12 = (bf16[128,1,2,128]{3,0,2,1:T(8,128)(2,1)S(1)}, bf16[128,1,2,128]{3,0,2,1:T(8,128)(2,1)S(1)}, u32[]{:S(2)}, u32[]{:S(2)}) collective-permute-start(bf16[128,1,2,128]{3,0,2,1:T(8,128)(2,1)S(1)} %get-tuple-element.121), channel_id=1, source_target_pairs={{0,11},{1,10},{2,9},{3,8},{4,15},{5,14},{6,13},{7,12},{8,3},{9,2},... | collective-permute-start | bytes 196616 | tf_op jit(solution)/shard_map/ppermute | solution.py:28
  299.1 23.8 %collective-permute-start.13 = (bf16[128,1,2,128]{3,0,2,1:T(8,128)(2,1)S(1)}, bf16[128,1,2,128]{3,0,2,1:T(8,128)(2,1)S(1)}, u32[]{:S(2)}, u32[]{:S(2)}) collective-permute-start(bf16[128,1,2,128]{3,0,2,1:T(8,128)(2,1)S(1)} %get-tuple-element.120), channel_id=1, source_target_pairs={{0,12},{1,13},{2,14},{3,15},{4,8},{5,9},{6,10},{7,11},{8,4},{9,5},... | collective-permute-start | bytes 196616 | tf_op jit(solution)/shard_map/ppermute | solution.py:28
  301.0 24.8 %collective-permute-start.14 = (bf16[128,1,2,128]{3,0,2,1:T(8,128)(2,1)S(1)}, bf16[128,1,2,128]{3,0,2,1:T(8,128)(2,1)S(1)}, u32[]{:S(2)}, u32[]{:S(2)}) collective-permute-start(bf16[128,1,2,128]{3,0,2,1:T(8,128)(2,1)S(1)} %get-tuple-element.119), channel_id=1, source_target_pairs={{0,13},{1,12},{2,15},{3,14},{4,9},{5,8},{6,11},{7,10},{8,5},{9,4},... | collective-permute-start | bytes 196616 | tf_op jit(solution)/shard_map/ppermute | solution.py:28
  304.9 22.3 %collective-permute-start.15 = (bf16[128,1,2,128]{3,0,2,1:T(8,128)(2,1)S(1)}, bf16[128,1,2,128]{3,0,2,1:T(8,128)(2,1)S(1)}, u32[]{:S(2)}, u32[]{:S(2)}) collective-permute-start(bf16[128,1,2,128]{3,0,2,1:T(8,128)(2,1)S(1)} %get-tuple-element.118), channel_id=1, source_target_pairs={{0,14},{1,15},{2,12},{3,13},{4,10},{5,11},{6,8},{7,9},{8,6},{9,7},... | collective-permute-start | bytes 196616 | tf_op jit(solution)/shard_map/ppermute | solution.py:28
  310.4 19.1 %collective-permute-start.16 = (bf16[128,1,2,128]{3,0,2,1:T(8,128)(2,1)S(1)}, bf16[128,1,2,128]{3,0,2,1:T(8,128)(2,1)S(1)}, u32[]{:S(2)}, u32[]{:S(2)}) collective-permute-start(bf16[128,1,2,128]{3,0,2,1:T(8,128)(2,1)S(1)} %get-tuple-element.117), channel_id=1, source_target_pairs={{0,15},{1,14},{2,13},{3,12},{4,11},{5,10},{6,9},{7,8},{8,7},{9,6},... | collective-permute-start | bytes 196616 | tf_op jit(solution)/shard_map/ppermute | solution.py:28
Sparse Core Ops, SparseCore 0:
  11.0 68.2 reduce-scatter.1
  98.8 80.0 all-gather.1
